TPU v7x, 768 devices: a whole 4x8x12 slice. The times are simulated.
768 devices in a mesh: blk: 192 (over x_lo, y, z), group: 4 (over x_hi, core).
Axes of the slice: x: 4 (x_hi: 2, x_lo: 2; x = x_hi * 2 + x_lo), y: 8, z: 12, core: 2. Of those that a mesh axis runs over, the one named last changes fastest.
Arguments:
- photo_features: float32 [122880, 1152], P(('blk', 'group')), may hold values from -0.1875 to 0.1875
- text_emb: float32 [122880, 1152], P(('blk', 'group')), may hold values from -0.1875 to 0.1875
- sharpness_factor: float32 [1], replicated, may hold values from 30 to 100
- logit_bias: float32 [1], replicated, may hold values from -6 to -2
Outputs:
- photo_feature_derivative: float32 [122880, 1152], P(('blk', 'group'))
- sentence_feature_derivative: float32 [122880, 1152], P(('blk', 'group'))
All inputs are finite; a program needn't handle non-finite values.
Results may differ from a plain program's by a relative error of at most 0.0003.
Values sent between devices are 32-bit elements; how exact they have to be, the bound alone decides.
No kernel may reach another device: no remote copies, remote signals or barrier semaphores. Data moves between devices by JAX's collectives and lax.ppermute only.
A program may use at most 64 MiB of HBM per device.

v0:
```python
import jax
import jax.numpy as jnp
from jax import lax
from jax.sharding import PartitionSpec as P


def extended(block, sides, width):
    for axis, dim in sides:
        count = lax.axis_size(axis)
        forward = [(i, i + 1) for i in range(count - 1)]
        forward.append((count - 1, 0))
        backward = [(target, source) for source, target in forward]
        low = lax.ppermute(
            lax.slice_in_dim(block, block.shape[dim] - width, None, axis=dim), axis, forward
        )
        high = lax.ppermute(lax.slice_in_dim(block, 0, width, axis=dim), axis, backward)
        block = jnp.concatenate([low, block, high], axis=dim)
    return block


def cross_similarity_derivatives(
    left_operand_features,
    right_operand_features,
    scaled_sharpness,
    segment_offset,
    opening_entry_index,
):
    similarity_matrix = (
        scaled_sharpness
        * jnp.dot(
            left_operand_features,
            right_operand_features.T,
            precision=lax.Precision.HIGHEST,
            preferred_element_type=jnp.float32,
        )
        + segment_offset
    )
    block_rows = right_operand_features.shape[0] // 3
    row_ids = (
        jnp.arange(left_operand_features.shape[0], dtype=jnp.int32)[:, None] + opening_entry_index
    )
    col_ids = jnp.arange(right_operand_features.shape[0], dtype=jnp.int32)[None, :]
    match_polarity = jnp.where(row_ids + block_rows == col_ids, jnp.float32(1.0), jnp.float32(-1.0))
    return -match_polarity * jax.nn.sigmoid(-match_polarity * similarity_matrix) * scaled_sharpness


def shards(photo_features, text_emb, sharpness_factor, logit_bias):
    row_count = photo_features.shape[0]
    block_rows = row_count * lax.axis_size("group")
    scaled_sharpness = sharpness_factor[0]
    segment_offset = logit_bias[0]
    opening_entry_index = lax.axis_index("group") * row_count
    text_block = lax.all_gather(text_emb, "group", axis=0, tiled=True)
    sentence_neighbourhood = extended(text_block, (("blk", 0),), block_rows)
    objective_derivatives = cross_similarity_derivatives(
        photo_features,
        sentence_neighbourhood,
        scaled_sharpness,
        segment_offset,
        opening_entry_index,
    )
    photo_feature_derivative = jnp.dot(
        objective_derivatives,
        sentence_neighbourhood,
        precision=lax.Precision.HIGHEST,
        preferred_element_type=jnp.float32,
    )
    partial_value = lax.dot_general(
        objective_derivatives,
        photo_features,
        (((0,), (0,)), ((), ())),
        precision=lax.Precision.HIGHEST,
        preferred_element_type=jnp.float32,
    )
    outward = jnp.concatenate([partial_value[:block_rows], partial_value[2 * block_rows :]], axis=0)
    returned = extended(outward, (("blk", 0),), block_rows)
    own_total = (
        partial_value[block_rows : 2 * block_rows]
        + returned[:block_rows]
        + returned[3 * block_rows :]
    )
    sentence_feature_derivative = lax.psum_scatter(
        own_total, "group", scatter_dimension=0, tiled=True
    )
    return (photo_feature_derivative, sentence_feature_derivative)


def solution(mesh):
    in_specs = (P(("blk", "group"), None), P(("blk", "group"), None), P(), P())
    out_specs = (P(("blk", "group"), None), P(("blk", "group"), None))
    return jax.shard_map(shards, mesh=mesh, in_specs=in_specs, out_specs=out_specs, check_vma=False)
```

profile of v0, /device:TPU:1, one launch (start us, length us, event | category | flops | bytes accessed | tf_op | source)
XLA Modules:
  0.0 288.4 jit_solution(14255038918685136514)
XLA Ops:
  7.2 0.0 copy-start
  7.2 0.0 all-gather.2.cloned.1.call-start
  7.2 0.7 all-gather.2.cloned.1.call-update
  7.9 0.0 reduce-scatter.2.cloned.1.call-start
  8.0 50.0 %all-gather.2.cloned.1.call-done = f32[640,1152]{1,0:T(8,128)} async-done(((f32[160,1152]{1,0:T(8,128)}), f32[640,1152]{1,0:T(8,128)}) %all-gather.2.cloned.1.call-update) | async-done | bytes 2949136 | tf_op jit(solution)/shard_map/all_gather | solution.py:53
  57.9 3.3 %collective-permute-start = (f32[640,1152]{1,0:T(8,128)}, f32[640,1152]{1,0:T(8,128)}, u32[]{:S(2)}, u32[]{:S(2)}) collective-permute-start(f32[640,1152]{1,0:T(8,128)} %all-gather.2.cloned.1.call-done), channel_id=1, source_target_pairs={{0,4},{4,8},{8,12},{12,16},{16,20},{20,24},{24,28},{28,32},{32,36}... | collective-permute-start | bytes 8847368 | tf_op jit(solution)/shard_map/ppermute | solution.py:13
  61.2 7.2 %collective-permute-start.1 = (f32[640,1152]{1,0:T(8,128)}, f32[640,1152]{1,0:T(8,128)}, u32[]{:S(2)}, u32[]{:S(2)}) collective-permute-start(f32[640,1152]{1,0:T(8,128)} %all-gather.2.cloned.1.call-done), channel_id=1, source_target_pairs={{4,0},{8,4},{12,8},{16,12},{20,16},{24,20},{28,24},{32,28},{36,32}... | collective-permute-start | bytes 8847368 | tf_op jit(solution)/shard_map/ppermute | solution.py:16
  69.8 0.0 copy-start.2
  69.8 61.1 %collective-permute-done = f32[640,1152]{1,0:T(8,128)} collective-permute-done((f32[640,1152]{1,0:T(8,128)}, f32[640,1152]{1,0:T(8,128)}, u32[]{:S(2)}, u32[]{:S(2)}) %collective-permute-start) | collective-permute-done | bytes 2949152 | tf_op jit(solution)/shard_map/ppermute | solution.py:13
  130.9 2.0 constant_dynamic-update-slice_fusion.2
  132.9 0.0 copy-done.2
  132.9 0.2 constant_dynamic-update-slice_fusion.1
  133.1 0.0 collective-permute-done.1
  133.1 2.0 constant_dynamic-update-slice_fusion
  135.2 0.0 copy-start.1
  135.2 0.0 copy-done
  135.2 8.8 %fusion.9 = f32[160,1920]{1,0:T(8,128)S(1)} fusion(f32[1920,1152]{1,0:T(8,128)S(1)} %constant_dynamic-update-slice_fusion, f32[160,1152]{1,0:T(8,128)S(1)} %copy-done, f32[]{:T(128)} %bitcast.24, f32[]{:T(128)} %bitcast.25, s32[160]{0:T(256)S(1)} %add_add_fusion), kind=kOutput, calls=%fused_computation.11 | convolution fusion | flops 4250112000 | bytes 10814088 | tf_op jit(solution)/shard_map/dot_general | solution.py:30
  144.0 0.0 copy-done.1
  144.0 9.2 %fusion.12 = f32[1920,1152]{1,0:T(8,128)S(1)} fusion(f32[160,1920]{1,0:T(8,128)S(1)} %fusion.9, f32[160,1152]{1,0:T(8,128)S(1)} %copy-done), kind=kOutput, calls=%fused_computation.19 | convolution fusion | flops 4246732800 | bytes 10813440 | tf_op jit(solution)/shard_map/dot_general | solution.py:68
  153.2 0.4 fusion.10
  153.6 6.9 %collective-permute-start.3 = (f32[640,1152]{1,0:T(8,128)S(1)}, f32[640,1152]{1,0:T(8,128)S(1)}, u32[]{:S(2)}, u32[]{:S(2)}) collective-permute-start(f32[640,1152]{1,0:T(8,128)S(1)} %get-tuple-element.3), channel_id=1, source_target_pairs={{4,0},{8,4},{12,8},{16,12},{20,16},{24,20},{28,24},{32,28},{36,32}... | collective-permute-start | bytes 8847368 | tf_op jit(solution)/shard_map/ppermute | solution.py:16
  160.5 1.9 collective-permute-start.2
  162.5 60.1 %collective-permute-done.3 = f32[640,1152]{1,0:T(8,128)S(1)} collective-permute-done((f32[640,1152]{1,0:T(8,128)S(1)}, f32[640,1152]{1,0:T(8,128)S(1)}, u32[]{:S(2)}, u32[]{:S(2)}) %collective-permute-start.3) | collective-permute-done | bytes 2949152 | tf_op jit(solution)/shard_map/ppermute | solution.py:16
  222.6 8.1 %collective-permute-done.2 = f32[640,1152]{1,0:T(8,128)S(1)} collective-permute-done((f32[640,1152]{1,0:T(8,128)S(1)}, f32[640,1152]{1,0:T(8,128)S(1)}, u32[]{:S(2)}, u32[]{:S(2)}) %collective-permute-start.2) | collective-permute-done | bytes 2949152 | tf_op jit(solution)/shard_map/ppermute | solution.py:13
  230.7 2.0 fusion
  232.7 0.0 reduce-scatter.2.cloned.1.call-update
  232.7 9.3 %fusion.11 = f32[160,1152]{1,0:T(8,128)} fusion(f32[160,1920]{1,0:T(8,128)S(1)} %fusion.9, f32[1920,1152]{1,0:T(8,128)} %copy-done.1), kind=kOutput, calls=%fused_computation.18 | convolution fusion | flops 4246732800 | bytes 10813440 | tf_op jit(solution)/shard_map/dot_general | solution.py:62
  242.0 39.5 %reduce-scatter.2.cloned.1.call-done = f32[160,1152]{1,0:T(8,128)} async-done(((f32[640,1152]{1,0:T(8,128)}), f32[160,1152]{1,0:T(8,128)}) %reduce-scatter.2.cloned.1.call-update) | async-done | bytes 737296 | tf_op jit(solution)/shard_map/reduce_scatter | solution.py:82
  (1 shorter events, 0.0 us)
Async XLA Ops:
  7.2 128.0 %copy-start = (f32[160,1152]{1,0:T(8,128)S(1)}, f32[160,1152]{1,0:T(8,128)}, u32[]{:S(2)}) copy-start(f32[160,1152]{1,0:T(8,128)} %param.4) | copy-start | bytes 2211844
  7.2 50.8 %all-gather.2.cloned.1.call-start = ((), (), s32[]{:S(2)}) async-start(), calls=%async_computation.1 | async-start | bytes 3686400 | tf_op jit(solution)/shard_map/all_gather | solution.py:53
  7.9 273.7 %reduce-scatter.2.cloned.1.call-start = ((), (), s32[]{:S(2)}) async-start(), calls=%async_computation.2 | async-start | bytes 3686400 | tf_op jit(solution)/shard_map/reduce_scatter | solution.py:82
  57.9 73.0 %collective-permute-start = (f32[640,1152]{1,0:T(8,128)}, f32[640,1152]{1,0:T(8,128)}, u32[]{:S(2)}, u32[]{:S(2)}) collective-permute-start(f32[640,1152]{1,0:T(8,128)} %all-gather.2.cloned.1.call-done), channel_id=1, source_target_pairs={{0,4},{4,8},{8,12},{12,16},{16,20},{20,24},{24,28},{28,32},{32,36}... | collective-permute-start | bytes 8847368 | tf_op jit(solution)/shard_map/ppermute | solution.py:13
  61.2 71.9 %collective-permute-start.1 = (f32[640,1152]{1,0:T(8,128)}, f32[640,1152]{1,0:T(8,128)}, u32[]{:S(2)}, u32[]{:S(2)}) collective-permute-start(f32[640,1152]{1,0:T(8,128)} %all-gather.2.cloned.1.call-done), channel_id=1, source_target_pairs={{4,0},{8,4},{12,8},{16,12},{20,16},{24,20},{28,24},{32,28},{36,32}... | collective-permute-start | bytes 8847368 | tf_op jit(solution)/shard_map/ppermute | solution.py:16
  69.8 63.2 %copy-start.2 = (f32[640,1152]{1,0:T(8,128)S(1)}, f32[640,1152]{1,0:T(8,128)}, u32[]{:S(2)}) copy-start(f32[640,1152]{1,0:T(8,128)} %all-gather.2.cloned.1.call-done) | copy-start | bytes 8847364
  135.2 8.8 %copy-start.1 = (f32[1920,1152]{1,0:T(8,128)}, f32[1920,1152]{1,0:T(8,128)S(1)}, u32[]{:S(2)}) copy-start(f32[1920,1152]{1,0:T(8,128)S(1)} %constant_dynamic-update-slice_fusion) | copy-start | bytes 26542084
  153.6 69.0 %collective-permute-start.3 = (f32[640,1152]{1,0:T(8,128)S(1)}, f32[640,1152]{1,0:T(8,128)S(1)}, u32[]{:S(2)}, u32[]{:S(2)}) collective-permute-start(f32[640,1152]{1,0:T(8,128)S(1)} %get-tuple-element.3), channel_id=1, source_target_pairs={{4,0},{8,4},{12,8},{16,12},{20,16},{24,20},{28,24},{32,28},{36,32}... | collective-permute-start | bytes 8847368 | tf_op jit(solution)/shard_map/ppermute | solution.py:16
  160.5 70.1 %collective-permute-start.2 = (f32[640,1152]{1,0:T(8,128)S(1)}, f32[640,1152]{1,0:T(8,128)S(1)}, u32[]{:S(2)}, u32[]{:S(2)}) collective-permute-start(f32[640,1152]{1,0:T(8,128)S(1)} %get-tuple-element.2), channel_id=1, source_target_pairs={{0,4},{4,8},{8,12},{12,16},{16,20},{20,24},{24,28},{28,32},{32,36}... | collective-permute-start | bytes 8847368 | tf_op jit(solution)/shard_map/ppermute | solution.py:13
Sparse Core Ops, SparseCore 0:
  10.4 47.4 all-gather.1
  232.8 48.7 reduce-scatter.1
where the time goes:
time: 289 us; the launch traced here: 288 us
  waiting for transfers between devices  220 us (76%)
  matrix products  27.3 us (9%)
  starting transfers between devices  19.4 us (7%)
  between operations  15.5 us (5%)
  local copies, waits for them, and re-layouts  4.64 us (2%)
    ppermute x2, waiting for transfers between devices, extended(): lax.ppermute(lax.slice_in_dim(block, block.shape[dim] - width, None, axis...  69.2 us
    ppermute x2, waiting for transfers between devices, extended(): lax.ppermute(lax.slice_in_dim(block, 0, width, axis=dim), axis, backward)  60.1 us
    all_gather x1, waiting for transfers between devices, shards(): text_block = lax.all_gather(text_emb, 'group', axis=0, tiled=True)  50 us
    reduce_scatter x1, waiting for transfers between devices, shards(): lax.psum_scatter(own_total, 'group', scatter_dimension=0, tiled=True)  39.5 us
    ppermute x2, starting transfers between devices, extended(): lax.ppermute(lax.slice_in_dim(block, 0, width, axis=dim), axis, backward)  14.2 us
    dot_general x1, matrix products, shards(): jnp.dot(objective_derivatives, sentence_neighbourhood, precision=lax.Prec...  9.34 us
    dot_general x1, matrix products, shards(): lax.dot_general(objective_derivatives, photo_features, (((0,), (0,)), (()...  9.19 us
    dot_general x1, matrix products, cross_similarity_derivatives(): jnp.dot(left_operand_features, right_operand_features.T, precision=lax.Pr...  8.78 us
  transfers between devices with their start and end apart: 6, of which 5 were waited for; matrix products, arithmetic and copies ran while one was open for 4% of the time, Pallas kernels for 0%

commit v1 on v0

v1 whole, which is shorter than its diff:
```python
import jax
import jax.numpy as jnp
from jax import lax
from jax.sharding import PartitionSpec as P

AXES = ("blk", "group")


def routes(mesh):
    positions, members = mesh.shape["blk"], mesh.shape["group"]
    forward, across, sibling = [], [], []
    for b in range(positions):
        for g in range(members):
            half, core = divmod(g, 2)
            turn = (b + 1) % (positions // 2) == 0
            landing = (1 - half if turn and core == 1 else half) * 2 + core
            here = b * members + g
            forward.append((here, (b + 1) % positions * members + landing))
            across.append((here, b * members + (1 - half) * 2 + core))
            sibling.append((here, b * members + half * 2 + 1 - core))
    backward = [(target, source) for source, target in forward]
    return forward, backward, across, sibling


def dot(a, b, dims):
    return lax.dot_general(a, b, (dims, ((), ())), precision=lax.Precision.HIGH, preferred_element_type=jnp.float32)


def solution(mesh):
    forward, backward, across, sibling = routes(mesh)

    def move(x, pairs):
        return lax.ppermute(x, AXES, pairs)

    def shards(photo, text, sharpness, bias):
        rows = photo.shape[0]
        scale, offset = sharpness[0], bias[0]
        below = move(text, forward)
        above = move(text, backward)
        far = move(photo, across)
        near = move(photo, sibling)
        far_near = move(far, sibling)
        texts = jnp.concatenate([below, text, above], axis=0)
        r = jnp.arange(2 * rows, dtype=jnp.int32)[:, None]
        c = jnp.arange(3 * rows, dtype=jnp.int32)[None, :]
        match = r + rows == c

        def slopes(left, diagonal):
            logit = scale * dot(left, texts, ((1,), (1,))) + offset
            if diagonal:
                label = jnp.where(match & (r < rows), jnp.float32(1), jnp.float32(-1))
                return -label * jax.nn.sigmoid(-label * logit) * scale
            return jax.nn.sigmoid(logit) * scale

        far2 = jnp.concatenate([far, far_near], axis=0)
        near2 = jnp.concatenate([photo, near], axis=0)
        g_far = slopes(far2, False)
        p_far = dot(g_far, texts, ((1,), (0,)))
        far_near_back = move(p_far[rows:], sibling)
        far_back = move(p_far[:rows] + far_near_back, across)
        g_near = slopes(near2, True)
        g = jnp.concatenate([g_near, g_far], axis=0)
        p = jnp.concatenate([near2, far2], axis=0)
        t = dot(g, p, ((0,), (0,)))
        t_below = move(t[:rows], backward)
        t_above = move(t[2 * rows :], forward)
        p_near = dot(g_near, texts, ((1,), (0,)))
        near_back = move(p_near[rows:], sibling)
        return p_near[:rows] + near_back + far_back, t[rows : 2 * rows] + t_below + t_above

    spec = P(AXES, None)
    return jax.shard_map(shards, mesh=mesh, in_specs=(spec, spec, P(), P()), out_specs=(spec, spec), check_vma=False)
```

time: 289 us -> 97.9 us (0.34)
  waiting for transfers between devices: 220 us -> 28.6 us
  starting transfers between devices: 19.4 us -> 53.1 us
  matrix products: 27.3 us -> 10.1 us
  between operations: 15.5 us -> 2.14 us
  local copies, waits for them, and re-layouts: 4.64 us -> 1.47 us
    ppermute x4 -> x10, waiting for transfers between devices: 129 us -> 28.6 us  [move(): return lax.ppermute(x, AXES, pairs)]
    all_gather x1 -> x0, waiting for transfers between devices: 50 us -> none  [shards(): text_block = lax.all_gather(text_emb, 'group', axis=0, tiled=True)]
    reduce_scatter x1 -> x0, waiting for transfers between devices: 39.5 us -> none  [shards(): lax.psum_scatter(own_total, 'group', scatter_dimension=0, tiled=True)]
    ppermute x4 -> x10, starting transfers between devices: 19.4 us -> 53.1 us  [move(): return lax.ppermute(x, AXES, pairs)]
    dot_general x3 -> x5, matrix products: 27.3 us -> 10.1 us  [dot(): lax.dot_general(a, b, (dims, ((), ())), precision=lax.Precision.HIGH, pre...]
  transfers between devices with their start and end apart: 6 -> 10, of which waited for: 5 -> 5; matrix products, arithmetic and copies ran while one was open for 4% -> 10% of each run, Pallas kernels for 0% -> 0%
where the time goes in v1:
time: 97.9 us; the launch traced here: 97.5 us
  starting transfers between devices  53.1 us (54%)
  waiting for transfers between devices  28.6 us (29%)
  matrix products  10.1 us (10%)
  between operations  2.14 us (2%)
  other arithmetic  2.07 us (2%)
  local copies, waits for them, and re-layouts  1.47 us (2%)
    ppermute x10, starting transfers between devices, move(): return lax.ppermute(x, AXES, pairs)  53.1 us
    ppermute x10, waiting for transfers between devices, move(): return lax.ppermute(x, AXES, pairs)  28.6 us
    dot_general x5, matrix products, dot(): lax.dot_general(a, b, (dims, ((), ())), precision=lax.Precision.HIGH, pre...  10.1 us
  transfers between devices with their start and end apart: 10, of which 5 were waited for; matrix products, arithmetic and copies ran while one was open for 10% of the time, Pallas kernels for 0%

profile of v1, /device:TPU:1, one launch (start us, length us, event | category | flops | bytes accessed | tf_op | source)
XLA Modules:
  0.0 97.5 jit_solution(16440623128218270260)
XLA Ops:
  0.6 5.5 %collective-permute-start.4 = (f32[160,1152]{1,0:T(8,128)}, f32[160,1152]{1,0:T(8,128)S(1)}, u32[]{:S(2)}, u32[]{:S(2)}) collective-permute-start(f32[160,1152]{1,0:T(8,128)} %param.4), channel_id=1, source_target_pairs={{0,2},{1,3},{2,0},{3,1},{4,6},{5,7},{6,4},{7,5},{8,10},{9,11},{10,... | collective-permute-start | bytes 2211848 | tf_op jit(solution)/shard_map/ppermute | solution.py:33
  6.1 4.0 %collective-permute-start.1 = (f32[160,1152]{1,0:T(8,128)}, f32[160,1152]{1,0:T(8,128)S(1)}, u32[]{:S(2)}, u32[]{:S(2)}) collective-permute-start(f32[160,1152]{1,0:T(8,128)} %param.5), channel_id=1, source_target_pairs={{0,4},{1,5},{2,6},{3,7},{4,8},{5,9},{6,10},{7,11},{8,12},{9,13},{1... | collective-permute-start | bytes 2211848 | tf_op jit(solution)/shard_map/ppermute | solution.py:33
  10.1 15.7 %collective-permute-start.2 = (f32[160,1152]{1,0:T(8,128)}, f32[160,1152]{1,0:T(8,128)S(1)}, u32[]{:S(2)}, u32[]{:S(2)}) collective-permute-start(f32[160,1152]{1,0:T(8,128)} %param.5), channel_id=1, source_target_pairs={{4,0},{5,1},{6,2},{7,3},{8,4},{9,5},{10,6},{11,7},{12,8},{13,9},{1... | collective-permute-start | bytes 2211848 | tf_op jit(solution)/shard_map/ppermute | solution.py:33
  25.8 2.6 %collective-permute-start = (f32[160,1152]{1,0:T(8,128)}, f32[160,1152]{1,0:T(8,128)S(1)}, u32[]{:S(2)}, u32[]{:S(2)}) collective-permute-start(f32[160,1152]{1,0:T(8,128)} %param.4), channel_id=1, source_target_pairs={{0,1},{1,0},{2,3},{3,2},{4,5},{5,4},{6,7},{7,6},{8,9},{9,8},{10,11... | collective-permute-start | bytes 2211848 | tf_op jit(solution)/shard_map/ppermute | solution.py:33
  29.8 0.0 copy-start
  29.8 0.0 collective-permute-done.4
  29.8 2.1 %collective-permute-start.5 = (f32[160,1152]{1,0:T(8,128)S(1)}, f32[160,1152]{1,0:T(8,128)S(1)}, u32[]{:S(2)}, u32[]{:S(2)}) collective-permute-start(f32[160,1152]{1,0:T(8,128)S(1)} %collective-permute-done.4), channel_id=1, source_target_pairs={{0,1},{1,0},{2,3},{3,2},{4,5},{5,4},{6,7},{7,6},{8,9},{9,8},{10,11... | collective-permute-start | bytes 2211848 | tf_op jit(solution)/shard_map/ppermute | solution.py:33
  31.9 7.9 %collective-permute-done.1 = f32[160,1152]{1,0:T(8,128)S(1)} collective-permute-done((f32[160,1152]{1,0:T(8,128)}, f32[160,1152]{1,0:T(8,128)S(1)}, u32[]{:S(2)}, u32[]{:S(2)}) %collective-permute-start.1) | collective-permute-done | bytes 737312 | tf_op jit(solution)/shard_map/ppermute | solution.py:33
  39.8 1.2 %constant_dynamic-update-slice_fusion.1 = f32[480,1152]{1,0:T(8,128)S(1)} fusion(f32[480,1152]{1,0:T(8,128)S(1)} %constant_dynamic-update-slice_fusion.2, f32[160,1152]{1,0:T(8,128)} %param.5), kind=kLoop, calls=%fused_computation.43 | loop fusion | bytes 1474560
  40.9 0.7 collective-permute-done.2
  41.7 0.0 collective-permute-done
  41.7 0.0 copy-done
  41.7 1.8 %fusion.64 = f32[320,480]{1,0:T(8,128)S(1)} fusion(f32[480,1152]{1,0:T(8,128)S(1)} %constant_dynamic-update-slice_fusion, f32[160,1152]{1,0:T(8,128)S(1)} %collective-permute-done, f32[160,1152]{1,0:T(8,128)S(1)} %copy-done, f32[]{:T(128)} %bitcast.10, f32[]{:T(128)} %bitcast.9, s32[320]{0:T(512)S(1)} %iota_add_fusion, pred[320]{0:T(512)(128)(4,1)S(1)} %iota_compare_fusion.1), kind=kOutput, calls=%fused_computation.34 | convolution fusion | flops 1063895040 | bytes 4302408 | tf_op jit(solution)/shard_map/dot_general | solution.py:26
  43.5 0.0 collective-permute-done.5
  43.5 1.7 %fusion.37 = f32[320,480]{1,0:T(8,128)S(1)} fusion(f32[480,1152]{1,0:T(8,128)S(1)} %constant_dynamic-update-slice_fusion, f32[160,1152]{1,0:T(8,128)S(1)} %collective-permute-done.5, f32[160,1152]{1,0:T(8,128)S(1)} %collective-permute-done.4, f32[]{:T(128)} %bitcast.11, f32[]{:T(128)} %bitcast.8), kind=kOutput, calls=%fused_computation.25 | convolution fusion | flops 1062973440 | bytes 4300808 | tf_op jit(solution)/shard_map/dot_general | solution.py:26
  45.2 1.7 %fusion.75 = f32[320,1152]{1,0:T(8,128)S(1)} fusion(f32[320,480]{1,0:T(8,128)S(1)} %fusion.37, f32[480,1152]{1,0:T(8,128)S(1)} %constant_dynamic-update-slice_fusion), kind=kOutput, calls=%fused_computation.52 | convolution fusion | flops 1061683200 | bytes 4300800 | tf_op jit(solution)/shard_map/dot_general | solution.py:26
  46.9 3.2 %collective-permute-start.6 = (f32[160,1152]{1,0:T(8,128)S(1)}, f32[160,1152]{1,0:T(8,128)S(1)}, u32[]{:S(2)}, u32[]{:S(2)}) collective-permute-start(f32[160,1152]{1,0:T(8,128)S(1)} %slice.31), channel_id=1, source_target_pairs={{0,1},{1,0},{2,3},{3,2},{4,5},{5,4},{6,7},{7,6},{8,9},{9,8},{10,11... | collective-permute-start | bytes 2211848 | tf_op jit(solution)/shard_map/ppermute | solution.py:33
  50.1 3.3 %fusion = f32[480,1152]{1,0:T(8,128)S(1)} fusion(f32[160,1152]{1,0:T(8,128)S(1)} %collective-permute-done.5, f32[160,1152]{1,0:T(8,128)S(1)} %collective-permute-done.4, f32[160,1152]{1,0:T(8,128)S(1)} %collective-permute-done, f32[160,1152]{1,0:T(8,128)S(1)} %copy-done, f32[320,480]{1,0:T(8,128)S(1)} %fusion.37, f32[320,480]{1,0:T(8,128)S(1)} %fusion.64), kind=kOutput, calls=%fused_computation | convolution fusion | flops 2125885440 | bytes 6389760 | tf_op jit(solution)/shard_map/dot_general | solution.py:26
  53.4 0.1 fusion.73
  53.5 1.9 %collective-permute-start.9 = (f32[160,1152]{1,0:T(8,128)S(1)}, f32[160,1152]{1,0:T(8,128)S(1)}, u32[]{:S(2)}, u32[]{:S(2)}) collective-permute-start(f32[160,1152]{1,0:T(8,128)S(1)} %get-tuple-element.3), channel_id=1, source_target_pairs={{0,4},{1,5},{2,6},{3,7},{4,8},{5,9},{6,10},{7,11},{8,12},{9,13},{1... | collective-permute-start | bytes 2211848 | tf_op jit(solution)/shard_map/ppermute | solution.py:33
  55.4 12.4 %collective-permute-start.8 = (f32[160,1152]{1,0:T(8,128)S(1)}, f32[160,1152]{1,0:T(8,128)S(1)}, u32[]{:S(2)}, u32[]{:S(2)}) collective-permute-start(f32[160,1152]{1,0:T(8,128)S(1)} %get-tuple-element.2), channel_id=1, source_target_pairs={{4,0},{5,1},{6,2},{7,3},{8,4},{9,5},{10,6},{11,7},{12,8},{13,9},{1... | collective-permute-start | bytes 2211848 | tf_op jit(solution)/shard_map/ppermute | solution.py:33
  67.8 1.7 %fusion.74 = f32[320,1152]{1,0:T(8,128)S(1)} fusion(f32[320,480]{1,0:T(8,128)S(1)} %fusion.64, f32[480,1152]{1,0:T(8,128)S(1)} %constant_dynamic-update-slice_fusion), kind=kOutput, calls=%fused_computation.51 | convolution fusion | flops 1061683200 | bytes 4300800 | tf_op jit(solution)/shard_map/dot_general | solution.py:26
  69.6 1.9 %collective-permute-start.3 = (f32[160,1152]{1,0:T(8,128)S(1)}, f32[160,1152]{1,0:T(8,128)S(1)}, u32[]{:S(2)}, u32[]{:S(2)}) collective-permute-start(f32[160,1152]{1,0:T(8,128)S(1)} %slice.29), channel_id=1, source_target_pairs={{0,1},{1,0},{2,3},{3,2},{4,5},{5,4},{6,7},{7,6},{8,9},{9,8},{10,11... | collective-permute-start | bytes 2211848 | tf_op jit(solution)/shard_map/ppermute | solution.py:33
  71.5 0.0 collective-permute-done.6
  71.5 0.1 slice_add_fusion.1
  71.6 3.9 %collective-permute-start.7 = (f32[160,1152]{1,0:T(8,128)S(1)}, f32[160,1152]{1,0:T(8,128)S(1)}, u32[]{:S(2)}, u32[]{:S(2)}) collective-permute-start(f32[160,1152]{1,0:T(8,128)S(1)} %slice_add_fusion.1), channel_id=1, source_target_pairs={{0,2},{1,3},{2,0},{3,1},{4,6},{5,7},{6,4},{7,5},{8,10},{9,11},{10,... | collective-permute-start | bytes 2211848 | tf_op jit(solution)/shard_map/ppermute | solution.py:33
  75.5 6.5 %collective-permute-done.9 = f32[160,1152]{1,0:T(8,128)S(1)} collective-permute-done((f32[160,1152]{1,0:T(8,128)S(1)}, f32[160,1152]{1,0:T(8,128)S(1)}, u32[]{:S(2)}, u32[]{:S(2)}) %collective-permute-start.9) | collective-permute-done | bytes 737312 | tf_op jit(solution)/shard_map/ppermute | solution.py:33
  82.0 1.0 %collective-permute-done.8 = f32[160,1152]{1,0:T(8,128)S(1)} collective-permute-done((f32[160,1152]{1,0:T(8,128)S(1)}, f32[160,1152]{1,0:T(8,128)S(1)}, u32[]{:S(2)}, u32[]{:S(2)}) %collective-permute-start.8) | collective-permute-done | bytes 737312 | tf_op jit(solution)/shard_map/ppermute | solution.py:33
  83.0 1.0 %fusion.67 = f32[160,1152]{1,0:T(8,128)} fusion(f32[160,1152]{1,0:T(8,128)S(1)} %collective-permute-done.9, f32[160,1152]{1,0:T(8,128)S(1)} %collective-permute-done.8, f32[480,1152]{1,0:T(8,128)S(1)} %fusion), kind=kLoop, calls=%fused_computation.36 | loop fusion | flops 368640 | bytes 2949120 | tf_op jit(solution)/shard_map/add | solution.py:69
  84.0 0.0 collective-permute-done.3
  84.0 12.5 %collective-permute-done.7 = f32[160,1152]{1,0:T(8,128)S(1)} collective-permute-done((f32[160,1152]{1,0:T(8,128)S(1)}, f32[160,1152]{1,0:T(8,128)S(1)}, u32[]{:S(2)}, u32[]{:S(2)}) %collective-permute-start.7) | collective-permute-done | bytes 737312 | tf_op jit(solution)/shard_map/ppermute | solution.py:33
  96.5 1.0 %fusion.68 = f32[160,1152]{1,0:T(8,128)} fusion(f32[160,1152]{1,0:T(8,128)S(1)} %collective-permute-done.7, f32[160,1152]{1,0:T(8,128)S(1)} %collective-permute-done.3, f32[320,1152]{1,0:T(8,128)S(1)} %fusion.74), kind=kLoop, calls=%fused_computation.39 | loop fusion | flops 368640 | bytes 2949120 | tf_op jit(solution)/shard_map/add | solution.py:69
  (6 shorter events, 0.2 us)
Async XLA Ops:
  0.6 29.2 %collective-permute-start.4 = (f32[160,1152]{1,0:T(8,128)}, f32[160,1152]{1,0:T(8,128)S(1)}, u32[]{:S(2)}, u32[]{:S(2)}) collective-permute-start(f32[160,1152]{1,0:T(8,128)} %param.4), channel_id=1, source_target_pairs={{0,2},{1,3},{2,0},{3,1},{4,6},{5,7},{6,4},{7,5},{8,10},{9,11},{10,... | collective-permute-start | bytes 2211848 | tf_op jit(solution)/shard_map/ppermute | solution.py:33
  6.1 33.6 %collective-permute-start.1 = (f32[160,1152]{1,0:T(8,128)}, f32[160,1152]{1,0:T(8,128)S(1)}, u32[]{:S(2)}, u32[]{:S(2)}) collective-permute-start(f32[160,1152]{1,0:T(8,128)} %param.5), channel_id=1, source_target_pairs={{0,4},{1,5},{2,6},{3,7},{4,8},{5,9},{6,10},{7,11},{8,12},{9,13},{1... | collective-permute-start | bytes 2211848 | tf_op jit(solution)/shard_map/ppermute | solution.py:33
  10.1 31.5 %collective-permute-start.2 = (f32[160,1152]{1,0:T(8,128)}, f32[160,1152]{1,0:T(8,128)S(1)}, u32[]{:S(2)}, u32[]{:S(2)}) collective-permute-start(f32[160,1152]{1,0:T(8,128)} %param.5), channel_id=1, source_target_pairs={{4,0},{5,1},{6,2},{7,3},{8,4},{9,5},{10,6},{11,7},{12,8},{13,9},{1... | collective-permute-start | bytes 2211848 | tf_op jit(solution)/shard_map/ppermute | solution.py:33
  25.8 15.8 %collective-permute-start = (f32[160,1152]{1,0:T(8,128)}, f32[160,1152]{1,0:T(8,128)S(1)}, u32[]{:S(2)}, u32[]{:S(2)}) collective-permute-start(f32[160,1152]{1,0:T(8,128)} %param.4), channel_id=1, source_target_pairs={{0,1},{1,0},{2,3},{3,2},{4,5},{5,4},{6,7},{7,6},{8,9},{9,8},{10,11... | collective-permute-start | bytes 2211848 | tf_op jit(solution)/shard_map/ppermute | solution.py:33
  29.8 11.9 %copy-start = (f32[160,1152]{1,0:T(8,128)S(1)}, f32[160,1152]{1,0:T(8,128)}, u32[]{:S(2)}) copy-start(f32[160,1152]{1,0:T(8,128)} %param.4) | copy-start | bytes 2211844
  29.8 13.7 %collective-permute-start.5 = (f32[160,1152]{1,0:T(8,128)S(1)}, f32[160,1152]{1,0:T(8,128)S(1)}, u32[]{:S(2)}, u32[]{:S(2)}) collective-permute-start(f32[160,1152]{1,0:T(8,128)S(1)} %collective-permute-done.4), channel_id=1, source_target_pairs={{0,1},{1,0},{2,3},{3,2},{4,5},{5,4},{6,7},{7,6},{8,9},{9,8},{10,11... | collective-permute-start | bytes 2211848 | tf_op jit(solution)/shard_map/ppermute | solution.py:33
  46.9 24.6 %collective-permute-start.6 = (f32[160,1152]{1,0:T(8,128)S(1)}, f32[160,1152]{1,0:T(8,128)S(1)}, u32[]{:S(2)}, u32[]{:S(2)}) collective-permute-start(f32[160,1152]{1,0:T(8,128)S(1)} %slice.31), channel_id=1, source_target_pairs={{0,1},{1,0},{2,3},{3,2},{4,5},{5,4},{6,7},{7,6},{8,9},{9,8},{10,11... | collective-permute-start | bytes 2211848 | tf_op jit(solution)/shard_map/ppermute | solution.py:33
  53.5 28.5 %collective-permute-start.9 = (f32[160,1152]{1,0:T(8,128)S(1)}, f32[160,1152]{1,0:T(8,128)S(1)}, u32[]{:S(2)}, u32[]{:S(2)}) collective-permute-start(f32[160,1152]{1,0:T(8,128)S(1)} %get-tuple-element.3), channel_id=1, source_target_pairs={{0,4},{1,5},{2,6},{3,7},{4,8},{5,9},{6,10},{7,11},{8,12},{9,13},{1... | collective-permute-start | bytes 2211848 | tf_op jit(solution)/shard_map/ppermute | solution.py:33
  55.4 27.6 %collective-permute-start.8 = (f32[160,1152]{1,0:T(8,128)S(1)}, f32[160,1152]{1,0:T(8,128)S(1)}, u32[]{:S(2)}, u32[]{:S(2)}) collective-permute-start(f32[160,1152]{1,0:T(8,128)S(1)} %get-tuple-element.2), channel_id=1, source_target_pairs={{4,0},{5,1},{6,2},{7,3},{8,4},{9,5},{10,6},{11,7},{12,8},{13,9},{1... | collective-permute-start | bytes 2211848 | tf_op jit(solution)/shard_map/ppermute | solution.py:33
  69.6 14.4 %collective-permute-start.3 = (f32[160,1152]{1,0:T(8,128)S(1)}, f32[160,1152]{1,0:T(8,128)S(1)}, u32[]{:S(2)}, u32[]{:S(2)}) collective-permute-start(f32[160,1152]{1,0:T(8,128)S(1)} %slice.29), channel_id=1, source_target_pairs={{0,1},{1,0},{2,3},{3,2},{4,5},{5,4},{6,7},{7,6},{8,9},{9,8},{10,11... | collective-permute-start | bytes 2211848 | tf_op jit(solution)/shard_map/ppermute | solution.py:33
  71.6 24.9 %collective-permute-start.7 = (f32[160,1152]{1,0:T(8,128)S(1)}, f32[160,1152]{1,0:T(8,128)S(1)}, u32[]{:S(2)}, u32[]{:S(2)}) collective-permute-start(f32[160,1152]{1,0:T(8,128)S(1)} %slice_add_fusion.1), channel_id=1, source_target_pairs={{0,2},{1,3},{2,0},{3,1},{4,6},{5,7},{6,4},{7,5},{8,10},{9,11},{10,... | collective-permute-start | bytes 2211848 | tf_op jit(solution)/shard_map/ppermute | solution.py:33

commit v2 on v1

v2 whole, which is shorter than its diff:
```python
import jax
import jax.numpy as jnp
from jax import lax
from jax.sharding import PartitionSpec as P

AXES = ("blk", "group")


def routes(mesh):
    positions, members = mesh.shape["blk"], mesh.shape["group"]
    forward, across, sibling = [], [], []
    for b in range(positions):
        for g in range(members):
            half, core = divmod(g, 2)
            turn = (b + 1) % (positions // 2) == 0
            landing = (1 - half if turn and core == 1 else half) * 2 + core
            here = b * members + g
            forward.append((here, (b + 1) % positions * members + landing))
            across.append((here, b * members + (1 - half) * 2 + core))
            sibling.append((here, b * members + half * 2 + 1 - core))
    backward = [(target, source) for source, target in forward]
    return forward, backward, across, sibling


def dot(a, b, dims):
    return lax.dot_general(a, b, (dims, ((), ())), precision=lax.Precision.HIGH, preferred_element_type=jnp.float32)


def after(value, *earlier):
    return lax.optimization_barrier((value, *earlier))[0]


def solution(mesh):
    forward, backward, across, sibling = routes(mesh)

    def move(x, pairs):
        return lax.ppermute(x, AXES, pairs)

    def shards(photo, text, sharpness, bias):
        rows = photo.shape[0]
        scale, offset = sharpness[0], bias[0]
        text_f = move(text, forward)
        text_b = move(text, backward)
        far = move(photo, across)
        near = move(photo, sibling)
        far_near = move(far, sibling)
        p = jnp.concatenate([photo, near, far, far_near], axis=0)
        texts = jnp.concatenate([text, text_f, text_b], axis=0)
        r = jnp.arange(4 * rows, dtype=jnp.int32)[:, None]
        c = jnp.arange(3 * rows, dtype=jnp.int32)[None, :]
        label = jnp.where((r == c) & (r < rows), jnp.float32(1), jnp.float32(-1))
        logit = scale * dot(p, texts, ((1,), (1,))) + offset
        g = -label * jax.nn.sigmoid(-label * logit) * scale
        p_far = dot(g[2 * rows :], texts, ((1,), (0,)))
        far_near_back = move(p_far[rows:], sibling)
        t_b = dot(after(g, p_far)[:, 2 * rows :], p, ((0,), (0,)))
        b_back = move(t_b, forward)
        p_across = p_far[:rows] + after(far_near_back, t_b)
        far_back = move(p_across, across)
        g = after(g, p_across)
        p_near = dot(g[: 2 * rows], texts, ((1,), (0,)))
        near_back = move(p_near[rows:], sibling)
        t_f = dot(after(g, p_near)[:, rows : 2 * rows], p, ((0,), (0,)))
        f_back = move(t_f, backward)
        t_own = dot(after(g, t_f)[:, :rows], p, ((0,), (0,))) + b_back
        p_own = p_near[:rows] + near_back + after(far_back, t_own)
        return p_own, t_own + after(f_back, p_own)

    spec = P(AXES, None)
    return jax.shard_map(shards, mesh=mesh, in_specs=(spec, spec, P(), P()), out_specs=(spec, spec), check_vma=False)
```

time: 97.9 us -> 91.6 us (0.936)
  starting transfers between devices: 53.1 us -> 48.8 us
  waiting for transfers between devices: 28.6 us -> 24.5 us
  local copies, waits for them, and re-layouts: 1.47 us -> 2.68 us
    ppermute x10, starting transfers between devices: 53.1 us -> 48.8 us  [move(): return lax.ppermute(x, AXES, pairs)]
    ppermute x10, waiting for transfers between devices: 28.6 us -> 24.5 us  [move(): return lax.ppermute(x, AXES, pairs)]
    unnamed x4 -> x5, local copies, waits for them, and re-layouts: 1.22 us -> 2.48 us
    dot_general x5 -> x6, matrix products: 10.1 us -> 11 us  [dot(): lax.dot_general(a, b, (dims, ((), ())), precision=lax.Precision.HIGH, pre...]
    add x4 -> x3, other arithmetic: 2.06 us -> 1.99 us  [the longest x1 0.97 us: shards(): p_own = p_near[:rows] + near_back + after(far_back, t_own)]
where the time goes in v2:
time: 91.6 us; the launch traced here: 91.1 us
  starting transfers between devices  48.8 us (53%)
  waiting for transfers between devices  24.5 us (27%)
  matrix products  11 us (12%)
  local copies, waits for them, and re-layouts  2.68 us (3%)
  between operations  2.15 us (2%)
  other arithmetic  2 us (2%)
    ppermute x10, starting transfers between devices, move(): return lax.ppermute(x, AXES, pairs)  48.8 us
    ppermute x10, waiting for transfers between devices, move(): return lax.ppermute(x, AXES, pairs)  24.5 us
    dot_general x6, matrix products, dot(): lax.dot_general(a, b, (dims, ((), ())), precision=lax.Precision.HIGH, pre...  11 us
    unnamed x5, local copies, waits for them, and re-layouts  2.48 us
  transfers between devices with their start and end apart: 10, of which 5 were waited for; matrix products, arithmetic and copies ran while one was open for 10% of the time, Pallas kernels for 0%

profile of v2, /device:TPU:1, one launch (start us, length us, event | category | flops | bytes accessed | tf_op | source)
XLA Modules:
  0.0 91.1 jit_solution(12101018390884500653)
XLA Ops:
  0.6 5.5 %collective-permute-start.1 = (f32[160,1152]{1,0:T(8,128)}, f32[160,1152]{1,0:T(8,128)S(1)}, u32[]{:S(2)}, u32[]{:S(2)}) collective-permute-start(f32[160,1152]{1,0:T(8,128)} %param.4), channel_id=1, source_target_pairs={{0,2},{1,3},{2,0},{3,1},{4,6},{5,7},{6,4},{7,5},{8,10},{9,11},{10,... | collective-permute-start | bytes 2211848 | tf_op jit(solution)/shard_map/ppermute | solution.py:37
  6.1 8.9 %collective-permute-start = (f32[160,1152]{1,0:T(8,128)}, f32[160,1152]{1,0:T(8,128)S(1)}, u32[]{:S(2)}, u32[]{:S(2)}) collective-permute-start(f32[160,1152]{1,0:T(8,128)} %param.4), channel_id=1, source_target_pairs={{0,1},{1,0},{2,3},{3,2},{4,5},{5,4},{6,7},{7,6},{8,9},{9,8},{10,11... | collective-permute-start | bytes 2211848 | tf_op jit(solution)/shard_map/ppermute | solution.py:37
  15.0 1.9 %collective-permute-start.3 = (f32[160,1152]{1,0:T(8,128)}, f32[160,1152]{1,0:T(8,128)S(1)}, u32[]{:S(2)}, u32[]{:S(2)}) collective-permute-start(f32[160,1152]{1,0:T(8,128)} %param.5), channel_id=1, source_target_pairs={{0,4},{1,5},{2,6},{3,7},{4,8},{5,9},{6,10},{7,11},{8,12},{9,13},{1... | collective-permute-start | bytes 2211848 | tf_op jit(solution)/shard_map/ppermute | solution.py:37
  16.9 11.8 %collective-permute-start.4 = (f32[160,1152]{1,0:T(8,128)}, f32[160,1152]{1,0:T(8,128)S(1)}, u32[]{:S(2)}, u32[]{:S(2)}) collective-permute-start(f32[160,1152]{1,0:T(8,128)} %param.5), channel_id=1, source_target_pairs={{4,0},{5,1},{6,2},{7,3},{8,4},{9,5},{10,6},{11,7},{12,8},{13,9},{1... | collective-permute-start | bytes 2211848 | tf_op jit(solution)/shard_map/ppermute | solution.py:37
  30.0 1.2 %constant_dynamic-update-slice_fusion.6 = f32[480,1152]{1,0:T(8,128)S(1)} fusion(f32[160,1152]{1,0:T(8,128)} %param.5), kind=kLoop, calls=%fused_computation.30 | loop fusion | bytes 1474560
  31.2 1.2 %constant_dynamic-update-slice_fusion.3 = f32[640,1152]{1,0:T(8,128)S(1)} fusion(f32[160,1152]{1,0:T(8,128)} %param.4), kind=kLoop, calls=%fused_computation.27 | loop fusion | bytes 1474560
  32.4 0.0 collective-permute-done.1
  32.4 1.9 %collective-permute-start.2 = (f32[160,1152]{1,0:T(8,128)S(1)}, f32[160,1152]{1,0:T(8,128)S(1)}, u32[]{:S(2)}, u32[]{:S(2)}) collective-permute-start(f32[160,1152]{1,0:T(8,128)S(1)} %collective-permute-done.1), channel_id=1, source_target_pairs={{0,1},{1,0},{2,3},{3,2},{4,5},{5,4},{6,7},{7,6},{8,9},{9,8},{10,11... | collective-permute-start | bytes 2211848 | tf_op jit(solution)/shard_map/ppermute | solution.py:37
  34.3 0.0 collective-permute-done
  34.3 0.1 constant_dynamic-update-slice_fusion.2
  34.4 0.1 constant_dynamic-update-slice_fusion.1
  34.4 9.1 %collective-permute-done.3 = f32[160,1152]{1,0:T(8,128)S(1)} collective-permute-done((f32[160,1152]{1,0:T(8,128)}, f32[160,1152]{1,0:T(8,128)S(1)}, u32[]{:S(2)}, u32[]{:S(2)}) %collective-permute-start.3) | collective-permute-done | bytes 737312 | tf_op jit(solution)/shard_map/ppermute | solution.py:37
  43.6 1.7 %collective-permute-done.4 = f32[160,1152]{1,0:T(8,128)S(1)} collective-permute-done((f32[160,1152]{1,0:T(8,128)}, f32[160,1152]{1,0:T(8,128)S(1)}, u32[]{:S(2)}, u32[]{:S(2)}) %collective-permute-start.4) | collective-permute-done | bytes 737312 | tf_op jit(solution)/shard_map/ppermute | solution.py:37
  45.3 0.0 collective-permute-done.2
  45.3 0.1 constant_dynamic-update-slice_fusion
  45.4 3.2 %fusion.7 = f32[640,480]{0,1:T(8,128)S(1)} fusion(f32[640,1152]{1,0:T(8,128)S(1)} %constant_dynamic-update-slice_fusion, f32[480,1152]{1,0:T(8,128)S(1)} %constant_dynamic-update-slice_fusion.4, f32[]{:T(128)} %bitcast.10, f32[]{:T(128)} %bitcast.9, pred[640]{0:T(1024)(128)(4,1)S(1)} %iota_compare_fusion.1), kind=kOutput, calls=%fused_computation.9 | convolution fusion | flops 2127052800 | bytes 6390408 | tf_op jit(solution)/shard_map/dot_general | solution.py:26
  48.6 1.9 %fusion.10 = f32[320,1152]{1,0:T(8,128)S(1)} fusion(f32[480,1152]{1,0:T(8,128)S(1)} %constant_dynamic-update-slice_fusion.4, f32[640,480]{0,1:T(8,128)S(1)} %fusion.7), kind=kOutput, calls=%fused_computation.15 | convolution fusion | flops 1061683200 | bytes 4423680 | tf_op jit(solution)/shard_map/dot_general | solution.py:26
  50.6 2.2 %collective-permute-start.5 = (f32[160,1152]{1,0:T(8,128)S(1)}, f32[160,1152]{1,0:T(8,128)S(1)}, u32[]{:S(2)}, u32[]{:S(2)}) collective-permute-start(f32[160,1152]{1,0:T(8,128)S(1)} %slice.38), channel_id=1, source_target_pairs={{0,1},{1,0},{2,3},{3,2},{4,5},{5,4},{6,7},{7,6},{8,9},{9,8},{10,11... | collective-permute-start | bytes 2211848 | tf_op jit(solution)/shard_map/ppermute | solution.py:37
  52.8 1.4 %fusion.17 = f32[160,1152]{1,0:T(8,128)S(1)} fusion(f32[640,1152]{1,0:T(8,128)S(1)} %constant_dynamic-update-slice_fusion, f32[640,480]{0,1:T(8,128)S(1)} %fusion.7), kind=kOutput, calls=%fused_computation.22 | convolution fusion | flops 707788800 | bytes 4096000 | tf_op jit(solution)/shard_map/dot_general | solution.py:26
  54.2 1.9 %collective-permute-start.8 = (f32[160,1152]{1,0:T(8,128)S(1)}, f32[160,1152]{1,0:T(8,128)S(1)}, u32[]{:S(2)}, u32[]{:S(2)}) collective-permute-start(f32[160,1152]{1,0:T(8,128)S(1)} %fusion.17), channel_id=1, source_target_pairs={{0,4},{1,5},{2,6},{3,7},{4,8},{5,9},{6,10},{7,11},{8,12},{9,13},{1... | collective-permute-start | bytes 2211848 | tf_op jit(solution)/shard_map/ppermute | solution.py:37
  56.1 0.0 collective-permute-done.5
  56.1 0.1 slice_add_fusion.1
  56.2 3.3 %collective-permute-start.7 = (f32[160,1152]{1,0:T(8,128)S(1)}, f32[160,1152]{1,0:T(8,128)S(1)}, u32[]{:S(2)}, u32[]{:S(2)}) collective-permute-start(f32[160,1152]{1,0:T(8,128)S(1)} %slice_add_fusion.1), channel_id=1, source_target_pairs={{0,2},{1,3},{2,0},{3,1},{4,6},{5,7},{6,4},{7,5},{8,10},{9,11},{10,... | collective-permute-start | bytes 2211848 | tf_op jit(solution)/shard_map/ppermute | solution.py:37
  59.5 1.7 %fusion.12 = f32[320,1152]{1,0:T(8,128)S(1)} fusion(f32[480,1152]{1,0:T(8,128)S(1)} %constant_dynamic-update-slice_fusion.4, f32[640,480]{0,1:T(8,128)S(1)} %fusion.7), kind=kOutput, calls=%fused_computation.17 | convolution fusion | flops 1061683200 | bytes 4423680 | tf_op jit(solution)/shard_map/dot_general | solution.py:26
  61.3 2.2 %collective-permute-start.6 = (f32[160,1152]{1,0:T(8,128)S(1)}, f32[160,1152]{1,0:T(8,128)S(1)}, u32[]{:S(2)}, u32[]{:S(2)}) collective-permute-start(f32[160,1152]{1,0:T(8,128)S(1)} %slice.40), channel_id=1, source_target_pairs={{0,1},{1,0},{2,3},{3,2},{4,5},{5,4},{6,7},{7,6},{8,9},{9,8},{10,11... | collective-permute-start | bytes 2211848 | tf_op jit(solution)/shard_map/ppermute | solution.py:37
  63.5 1.4 %fusion.15 = f32[160,1152]{1,0:T(8,128)S(1)} fusion(f32[640,1152]{1,0:T(8,128)S(1)} %constant_dynamic-update-slice_fusion, f32[640,480]{0,1:T(8,128)S(1)} %fusion.7), kind=kOutput, calls=%fused_computation.20 | convolution fusion | flops 707788800 | bytes 4096000 | tf_op jit(solution)/shard_map/dot_general | solution.py:26
  64.9 9.2 %collective-permute-start.9 = (f32[160,1152]{1,0:T(8,128)S(1)}, f32[160,1152]{1,0:T(8,128)S(1)}, u32[]{:S(2)}, u32[]{:S(2)}) collective-permute-start(f32[160,1152]{1,0:T(8,128)S(1)} %fusion.15), channel_id=1, source_target_pairs={{4,0},{5,1},{6,2},{7,3},{8,4},{9,5},{10,6},{11,7},{12,8},{13,9},{1... | collective-permute-start | bytes 2211848 | tf_op jit(solution)/shard_map/ppermute | solution.py:37
  74.1 5.7 %collective-permute-done.8 = f32[160,1152]{1,0:T(8,128)S(1)} collective-permute-done((f32[160,1152]{1,0:T(8,128)S(1)}, f32[160,1152]{1,0:T(8,128)S(1)}, u32[]{:S(2)}, u32[]{:S(2)}) %collective-permute-start.8) | collective-permute-done | bytes 737312 | tf_op jit(solution)/shard_map/ppermute | solution.py:37
  79.8 1.4 %convolution_add_fusion = f32[160,1152]{1,0:T(8,128)S(1)} fusion(f32[160,1152]{1,0:T(8,128)S(1)} %collective-permute-done.8, f32[640,1152]{1,0:T(8,128)S(1)} %constant_dynamic-update-slice_fusion, f32[640,480]{0,1:T(8,128)S(1)} %fusion.7), kind=kOutput, calls=%fused_computation | convolution fusion | flops 707973120 | bytes 4833280 | tf_op jit(solution)/shard_map/dot_general | solution.py:26
  81.2 4.2 %collective-permute-done.7 = f32[160,1152]{1,0:T(8,128)S(1)} collective-permute-done((f32[160,1152]{1,0:T(8,128)S(1)}, f32[160,1152]{1,0:T(8,128)S(1)}, u32[]{:S(2)}, u32[]{:S(2)}) %collective-permute-start.7) | collective-permute-done | bytes 737312 | tf_op jit(solution)/shard_map/ppermute | solution.py:37
  85.4 0.0 collective-permute-done.6
  85.4 1.0 %fusion.9 = f32[160,1152]{1,0:T(8,128)} fusion(f32[160,1152]{1,0:T(8,128)S(1)} %collective-permute-done.7, f32[160,1152]{1,0:T(8,128)S(1)} %collective-permute-done.6, f32[320,1152]{1,0:T(8,128)S(1)} %fusion.12), kind=kLoop, calls=%fused_computation.13 | loop fusion | flops 368640 | bytes 2949120 | tf_op jit(solution)/shard_map/add | solution.py:66
  86.4 3.8 %collective-permute-done.9 = f32[160,1152]{1,0:T(8,128)S(1)} collective-permute-done((f32[160,1152]{1,0:T(8,128)S(1)}, f32[160,1152]{1,0:T(8,128)S(1)}, u32[]{:S(2)}, u32[]{:S(2)}) %collective-permute-start.9) | collective-permute-done | bytes 737312 | tf_op jit(solution)/shard_map/ppermute | solution.py:37
  90.2 0.9 %add.31 = f32[160,1152]{1,0:T(8,128)} add(f32[160,1152]{1,0:T(8,128)S(1)} %convolution_add_fusion, f32[160,1152]{1,0:T(8,128)S(1)} %collective-permute-done.9) | non-fusion elementwise | flops 184320 | bytes 2211840 | tf_op jit(solution)/shard_map/add | solution.py:67
  (5 shorter events, 0.2 us)
Async XLA Ops:
  0.6 31.7 %collective-permute-start.1 = (f32[160,1152]{1,0:T(8,128)}, f32[160,1152]{1,0:T(8,128)S(1)}, u32[]{:S(2)}, u32[]{:S(2)}) collective-permute-start(f32[160,1152]{1,0:T(8,128)} %param.4), channel_id=1, source_target_pairs={{0,2},{1,3},{2,0},{3,1},{4,6},{5,7},{6,4},{7,5},{8,10},{9,11},{10,... | collective-permute-start | bytes 2211848 | tf_op jit(solution)/shard_map/ppermute | solution.py:37
  6.1 28.2 %collective-permute-start = (f32[160,1152]{1,0:T(8,128)}, f32[160,1152]{1,0:T(8,128)S(1)}, u32[]{:S(2)}, u32[]{:S(2)}) collective-permute-start(f32[160,1152]{1,0:T(8,128)} %param.4), channel_id=1, source_target_pairs={{0,1},{1,0},{2,3},{3,2},{4,5},{5,4},{6,7},{7,6},{8,9},{9,8},{10,11... | collective-permute-start | bytes 2211848 | tf_op jit(solution)/shard_map/ppermute | solution.py:37
  15.0 28.5 %collective-permute-start.3 = (f32[160,1152]{1,0:T(8,128)}, f32[160,1152]{1,0:T(8,128)S(1)}, u32[]{:S(2)}, u32[]{:S(2)}) collective-permute-start(f32[160,1152]{1,0:T(8,128)} %param.5), channel_id=1, source_target_pairs={{0,4},{1,5},{2,6},{3,7},{4,8},{5,9},{6,10},{7,11},{8,12},{9,13},{1... | collective-permute-start | bytes 2211848 | tf_op jit(solution)/shard_map/ppermute | solution.py:37
  16.9 28.3 %collective-permute-start.4 = (f32[160,1152]{1,0:T(8,128)}, f32[160,1152]{1,0:T(8,128)S(1)}, u32[]{:S(2)}, u32[]{:S(2)}) collective-permute-start(f32[160,1152]{1,0:T(8,128)} %param.5), channel_id=1, source_target_pairs={{4,0},{5,1},{6,2},{7,3},{8,4},{9,5},{10,6},{11,7},{12,8},{13,9},{1... | collective-permute-start | bytes 2211848 | tf_op jit(solution)/shard_map/ppermute | solution.py:37
  32.4 12.9 %collective-permute-start.2 = (f32[160,1152]{1,0:T(8,128)S(1)}, f32[160,1152]{1,0:T(8,128)S(1)}, u32[]{:S(2)}, u32[]{:S(2)}) collective-permute-start(f32[160,1152]{1,0:T(8,128)S(1)} %collective-permute-done.1), channel_id=1, source_target_pairs={{0,1},{1,0},{2,3},{3,2},{4,5},{5,4},{6,7},{7,6},{8,9},{9,8},{10,11... | collective-permute-start | bytes 2211848 | tf_op jit(solution)/shard_map/ppermute | solution.py:37
  50.6 5.5 %collective-permute-start.5 = (f32[160,1152]{1,0:T(8,128)S(1)}, f32[160,1152]{1,0:T(8,128)S(1)}, u32[]{:S(2)}, u32[]{:S(2)}) collective-permute-start(f32[160,1152]{1,0:T(8,128)S(1)} %slice.38), channel_id=1, source_target_pairs={{0,1},{1,0},{2,3},{3,2},{4,5},{5,4},{6,7},{7,6},{8,9},{9,8},{10,11... | collective-permute-start | bytes 2211848 | tf_op jit(solution)/shard_map/ppermute | solution.py:37
  54.2 25.7 %collective-permute-start.8 = (f32[160,1152]{1,0:T(8,128)S(1)}, f32[160,1152]{1,0:T(8,128)S(1)}, u32[]{:S(2)}, u32[]{:S(2)}) collective-permute-start(f32[160,1152]{1,0:T(8,128)S(1)} %fusion.17), channel_id=1, source_target_pairs={{0,4},{1,5},{2,6},{3,7},{4,8},{5,9},{6,10},{7,11},{8,12},{9,13},{1... | collective-permute-start | bytes 2211848 | tf_op jit(solution)/shard_map/ppermute | solution.py:37
  56.2 29.2 %collective-permute-start.7 = (f32[160,1152]{1,0:T(8,128)S(1)}, f32[160,1152]{1,0:T(8,128)S(1)}, u32[]{:S(2)}, u32[]{:S(2)}) collective-permute-start(f32[160,1152]{1,0:T(8,128)S(1)} %slice_add_fusion.1), channel_id=1, source_target_pairs={{0,2},{1,3},{2,0},{3,1},{4,6},{5,7},{6,4},{7,5},{8,10},{9,11},{10,... | collective-permute-start | bytes 2211848 | tf_op jit(solution)/shard_map/ppermute | solution.py:37
  61.3 24.1 %collective-permute-start.6 = (f32[160,1152]{1,0:T(8,128)S(1)}, f32[160,1152]{1,0:T(8,128)S(1)}, u32[]{:S(2)}, u32[]{:S(2)}) collective-permute-start(f32[160,1152]{1,0:T(8,128)S(1)} %slice.40), channel_id=1, source_target_pairs={{0,1},{1,0},{2,3},{3,2},{4,5},{5,4},{6,7},{7,6},{8,9},{9,8},{10,11... | collective-permute-start | bytes 2211848 | tf_op jit(solution)/shard_map/ppermute | solution.py:37
  64.9 25.3 %collective-permute-start.9 = (f32[160,1152]{1,0:T(8,128)S(1)}, f32[160,1152]{1,0:T(8,128)S(1)}, u32[]{:S(2)}, u32[]{:S(2)}) collective-permute-start(f32[160,1152]{1,0:T(8,128)S(1)} %fusion.15), channel_id=1, source_target_pairs={{4,0},{5,1},{6,2},{7,3},{8,4},{9,5},{10,6},{11,7},{12,8},{13,9},{1... | collective-permute-start | bytes 2211848 | tf_op jit(solution)/shard_map/ppermute | solution.py:37
